TPU v7x, 128 devices: a whole 4x4x4 slice. The times are simulated.
128 devices in a mesh: ctx: 16 (over z, x), head: 2 (over y_hi), dp: 4 (over y_lo, core).
Axes of the slice: x: 4, y: 4 (y_hi: 2, y_lo: 2; y = y_hi * 2 + y_lo), z: 4, core: 2. Of those that a mesh axis runs over, the one named last changes fastest.
Arguments:
- queries: bfloat16 [4, 2048, 5120], P('dp', 'ctx', 'head'), may hold values from -200 to 200
- keys: bfloat16 [4, 16384, 1024], P('dp', 'ctx', 'head'), may hold values from -6 to 6
- start_block: int32 [4], P('dp'), may hold values from 0 to 224, as said below
- lengths: int32 [4], P('dp'), may hold values from 2048 to 16384, as said below
- gate_query: bfloat16 [8, 640, 128], P('head'), may hold values from -2 to 2
- gate_key: bfloat16 [8, 384, 128], P('head'), may hold values from -0.3125 to 0.3125
Outputs:
- grad_query: float32 [8, 640, 128], P('head')
- grad_key: float32 [8, 384, 128], P('head')
- block_loss: float32 [4, 8], P('dp', 'head')
Inputs may be any that keep to these rules, and one draw needn't show every extreme that they name: The span's 32 blocks lie inside the context: start_block + 32 <= 256. Every query token of the span lies before the sequence's length: lengths >= 64 * (start_block + 32).
All inputs are finite; a program needn't handle non-finite values.
Results may differ from a plain program's by a relative error of at most 0.0003.
Values may be sent and summed in bfloat16 or wider, within the bound.
No kernel may reach another device: no remote copies, remote signals or barrier semaphores. Data moves between devices by JAX's collectives and lax.ppermute only.
A program may use at most 320 MiB of HBM per device.

v0:
```python
import functools
import itertools
import math

import jax
import jax.numpy as jnp
from jax import lax
from jax.experimental import pallas as pl
from jax.experimental.pallas import tpu as pltpu
from jax.sharding import Mesh, PartitionSpec as P

BLK = 64
GROUP = 5
HD = 128
QB = 32
CB = 256
NEG = -1e30
FLOOR = -1e20
KT = 512
KB = KT // BLK
SAFE = 100.0
SCALE = HD ** -0.5
SCALE2 = SCALE * math.log2(math.e)
VMEM = 56 * 2 ** 20
F32 = jnp.float32
BF16 = jnp.bfloat16
NT = (((1,), (1,)), ((), ()))
TN = (((0,), (0,)), ((), ()))
NN = (((1,), (0,)), ((), ()))
PQ_AT = 256
START_AT = PQ_AT + 80
PACK = START_AT + 16


def split2(x):
    hi = x.astype(BF16)
    return hi, (x - hi.astype(F32)).astype(BF16)


def mm(a, b, dims=NN):
    return lax.dot_general(a, b, dims, preferred_element_type=F32)


def mm3(a, b, dims=NN):
    return mm(a[0], b[0], dims) + (mm(a[0], b[1], dims) + mm(a[1], b[0], dims))


def block_tops(s):
    return s.reshape(s.shape[0] // BLK, 8, 8, s.shape[1]).max(axis=1).max(axis=1)


def part_sums(s, m):
    return jnp.exp2(s - m).reshape(s.shape[0] // 8, 8, s.shape[1]).sum(axis=0)


def scores_kernel(pos_ref, *refs, n_q, shards):
    refs, nk = list(refs), len(shards)
    take = lambda n: [refs.pop(0) for _ in range(n)]
    q_refs, k_refs = take(n_q), take(nk)
    first = n_q > 1
    ml_in = [] if first else take(1)
    bm_ref, ml_ref = take(2)
    qs = take(1)[0] if first else q_refs[0]
    d_s, bad_s = refs
    rt, piece = qs.shape[2], k_refs[0].shape[0]
    q_pos = [pos_ref[i] for i in range(4)]
    kp = [pos_ref[4 + i] for i in shards]
    if first:
        for i, r in enumerate(q_refs):
            at = pl.multiple_of(pos_ref[8 + i], 128)
            for h in range(GROUP):
                hi, lo = split2(r[:, h * HD:(h + 1) * HD].astype(F32) * SCALE2)
                qs[0, h, pl.ds(at, 128), :] = jnp.concatenate([hi, lo], axis=1)
    tiles = [(p, o) for p in range(nk) for o in range(0, piece, KT)]
    low, high = functools.reduce(jnp.minimum, q_pos), functools.reduce(jnp.maximum, q_pos)
    full = [k + piece // BLK - 1 < low for k in kp]
    none = functools.reduce(jnp.minimum, kp) > high + 1

    def scores(t, h):
        p, o = tiles[t]
        k = k_refs[p][o:o + KT, :]
        return mm(jnp.concatenate([k, k], axis=1), qs[0, h], NT)

    def seen(p):
        lane = lax.broadcasted_iota(jnp.int32, (8, rt), 1)
        d = lane % 128 - lax.broadcasted_iota(jnp.int32, (8, rt), 0)
        for i, v in enumerate(q_pos):
            d = d + jnp.where(lane // 128 == i, (v - kp[p]) * BLK, 0)
        return d

    def masked(t, h):
        p, o = tiles[t]
        keep = jnp.concatenate([d_s[p] >= o + i for i in range(0, KT, 8)], axis=0)
        return jnp.where(keep, scores(t, h), NEG)

    def store(h, found):
        if ml_in:
            m = ml_in[0][0, h, 0:1, :]
            found = found + [(m, m, ml_in[0][0, h, 1:2, :])]
        big = functools.reduce(jnp.maximum, [f[1] for f in found])
        ml_ref[0, h, 0:1, :] = big
        ml_ref[0, h, 1:2, :] = sum(f[2] * jnp.exp2(f[0] - big) for f in found)

    def heads(masks):
        for p in range(nk):
            if masks[p]:
                d_s[p] = seen(p)

        def head(h, worst):
            found = []
            for t, (p, o) in enumerate(tiles):
                s = masked(t, h) if masks[p] else scores(t, h)
                if t == 0 or (o == 0 and (masks[p] or masks[p - 1])):
                    m = s[:BLK].reshape(8, 8, rt).max(axis=0).max(axis=0, keepdims=True)
                    m = jnp.maximum(m, FLOOR) if masks[p] else m
                    found.append([m, m, None])
                top, part = block_tops(s), part_sums(s, m)
                bm_ref[0, h, t * KB:(t + 1) * KB, :] = top
                f = found[-1]
                f[1] = jnp.maximum(f[1], top.max(axis=0, keepdims=True))
                f[2] = part if f[2] is None else f[2] + part
            store(h, [(f[0], f[1], f[2].sum(axis=0, keepdims=True)) for f in found])
            return functools.reduce(jnp.maximum, [f[1] - f[0] for f in found], worst)

        worst = jnp.zeros((1, rt), F32)
        if nk == 1 or not any(masks):
            for h in range(GROUP):
                worst = head(h, worst)
        else:
            worst = lax.fori_loop(0, GROUP, head, worst)
        bad_s[0] = jnp.max(worst)

    for masks in itertools.product((False, True), repeat=nk):
        match = functools.reduce(jnp.logical_and, [f != m for f, m in zip(full, masks)])
        pl.when(match & jnp.logical_not(none))(functools.partial(heads, masks))

    @pl.when(none)
    def _():
        bm_ref[...] = jnp.full(bm_ref.shape, NEG, F32)
        for h in range(GROUP):
            store(h, [(jnp.full((1, rt), FLOOR, F32), jnp.full((1, rt), FLOOR, F32), jnp.zeros((1, rt), F32))])
        bad_s[0] = 0.0

    @pl.when(bad_s[0] > SAFE)
    def _():
        for p in range(nk):
            d_s[p] = seen(p)

        def head(h, _):
            m, l = jnp.full((1, rt), FLOOR, F32), jnp.zeros((8, rt), F32)
            for t in range(len(tiles)):
                s = masked(t, h)
                top = block_tops(s)
                bm_ref[0, h, t * KB:(t + 1) * KB, :] = top
                new = jnp.maximum(m, top.max(axis=0, keepdims=True))
                l = l * jnp.exp2(m - new) + part_sums(s, new)
                m = new
            store(h, [(m, m, l.sum(axis=0, keepdims=True))])
            return 0

        lax.fori_loop(0, GROUP, head, 0)


def block_scores(pos, q_parts, k_parts, shards, ml_in=()):
    first = len(q_parts) > 1
    rt, kn = 512, sum(k.shape[0] for k in k_parts)
    groups = k_parts[0].shape[1] // HD
    per_group = lambda s: pl.BlockSpec((1,) + tuple(s[1:]), lambda g, p: (g, 0, 0, 0))
    lanes = lambda v: pl.BlockSpec((v.shape[0], v.shape[1] // groups), lambda g, p: (0, g))
    shapes = [(groups, GROUP, kn // BLK, rt), (groups, GROUP, 2, rt)] + [(groups, GROUP, rt, 2 * HD)] * first
    return pl.pallas_call(
        functools.partial(scores_kernel, n_q=len(q_parts), shards=shards),
        grid_spec=pltpu.PrefetchScalarGridSpec(
            num_scalar_prefetch=1,
            grid=(groups,),
            in_specs=[lanes(q) if first else per_group(q.shape) for q in q_parts]
            + [lanes(k) for k in k_parts]
            + [per_group(m.shape) for m in ml_in],
            out_specs=[per_group(s) for s in shapes],
            scratch_shapes=[pltpu.VMEM((len(k_parts), 8, rt), jnp.int32), pltpu.SMEM((1,), F32)],
        ),
        out_shape=[jax.ShapeDtypeStruct(s, t) for s, t in zip(shapes, (F32, F32, BF16))],
        compiler_params=pltpu.CompilerParams(vmem_limit_bytes=VMEM),
        name="block_scores",
    )(pos, *q_parts, *k_parts, *ml_in)


def pool_kernel(start_ref, q_ref, k_ref, out_ref):
    groups = k_ref.shape[1] // HD
    for g in range(groups):
        x = k_ref[:, g * HD:(g + 1) * HD].astype(F32).reshape(16, BLK, HD)
        hi, lo = split2(x.sum(axis=1) * (1.0 / BLK))
        parts = [x.max(axis=1).astype(BF16), x.min(axis=1).astype(BF16), hi, lo]
        for p, part in enumerate(parts):
            out_ref[g * 64 + p * 16:g * 64 + p * 16 + 16, :] = part
    for p in range(GROUP):
        rows = []
        for g in range(groups):
            at = (g * GROUP + p) * HD
            x = q_ref[:, at:at + HD].astype(F32).reshape(2, BLK, HD)
            rows.append(x.sum(axis=1) * (1.0 / BLK))
        hi, lo = split2(jnp.concatenate(rows, axis=0))
        at = PQ_AT + p * 16
        out_ref[at:at + 16, :] = jnp.concatenate([hi.astype(F32), lo.astype(F32)], axis=0).astype(BF16)
    out_ref[START_AT:, :] = jnp.full((16, HD), start_ref[0].astype(F32), F32).astype(BF16)


def pool(start_block, q, k):
    return pl.pallas_call(
        pool_kernel,
        in_specs=[
            pl.BlockSpec(memory_space=pltpu.SMEM),
            pl.BlockSpec(memory_space=pltpu.VMEM),
            pl.BlockSpec(memory_space=pltpu.VMEM),
        ],
        out_specs=pl.BlockSpec(memory_space=pltpu.VMEM),
        out_shape=jax.ShapeDtypeStruct((PACK, HD), BF16),
        compiler_params=pltpu.CompilerParams(vmem_limit_bytes=VMEM),
        name="pool",
    )(start_block, q, k)


def teacher_kernel(x_ref, *refs):
    near, sides, far = refs[:3]
    ml_refs, (out_ref, sc) = refs[3:-2], refs[-2:]
    rt = near.shape[3]
    to = [pl.multiple_of(((x_ref[0] + o) & 3) * 16, 16) for o in (0, 3, 1, 2)]
    for g in range(4):
        for h in range(GROUP):
            ms = [m[g, h, 0:1, :] for m in ml_refs]
            m = functools.reduce(jnp.maximum, ms)
            l = sum(ref[g, h, 1:2, :] * jnp.exp2(mi - m) for ref, mi in zip(ml_refs, ms))
            lse = m + jnp.log(l) * math.log2(math.e)
            parts = [near[g, h], sides[g, h, :16], sides[g, h, 16:], far[g, h]]
            for at, v in zip(to, parts):
                sc[g // 2 * GROUP + h, pl.ds(at + g % 2 * 64, 16), :] = v - lse
    for gp in range(2):
        totals = [None] * (rt // 128)
        for h in range(GROUP):
            for i in range(rt // 128):
                t = sc[gp * GROUP + h, :, i * 128:(i + 1) * 128].T
                top = jnp.exp2(t.reshape(2, BLK, 128).max(axis=1))
                totals[i] = top if h == 0 else totals[i] + top
        tile = jnp.concatenate(totals, axis=0) * (1.0 / GROUP)
        out_ref[:, gp] = jnp.broadcast_to(tile[None], (out_ref.shape[0],) + tile.shape)


def teacher_blocks(x, bms, mls, copies):
    return pl.pallas_call(
        teacher_kernel,
        in_specs=[pl.BlockSpec(memory_space=pltpu.SMEM)]
        + [pl.BlockSpec(memory_space=pltpu.VMEM)] * (len(bms) + len(mls)),
        out_specs=pl.BlockSpec(memory_space=pltpu.VMEM),
        out_shape=jax.ShapeDtypeStruct((copies, 2, 8, 128), F32),
        scratch_shapes=[pltpu.VMEM((2 * GROUP, 128, bms[0].shape[3]), F32)],
        compiler_params=pltpu.CompilerParams(vmem_limit_bytes=VMEM),
        name="teacher",
    )(x, *bms, *mls)


def packed(pack_ref, si, at):
    return pack_ref[:, :, si, pl.ds(at, 16), :].reshape(CB, HD)


def gate_kernel(at_ref, *refs):
    parts, (wq_ref, wk_ref) = refs[:4], refs[4:6]
    pack_ref, gate_ref, log_ref, xh_ref, xl_ref, kh_ref, kl_ref, qh_ref, ql_ref = refs[6:]
    gp = pl.program_id(0)

    @pl.when(gp == 0)
    def _():
        for i in range(4):
            for j in range(4):
                for si in range(2):
                    pack_ref[(at_ref[0] + i) & 3, (at_ref[1] + j) & 3, si] = parts[i][j, si]

    row = lax.broadcasted_iota(jnp.int32, (2 * QB, CB), 0)
    col = lax.broadcasted_iota(jnp.int32, (2 * QB, CB), 1)
    a = row % QB
    pick = (
        (col % 8 == (gp * 2 + row // QB) * 2 + a % 2)
        & (col // 16 % 4 == a // 8)
        & (col // 64 == a % 8 // 2)
    )
    pick = jnp.where(pick, 1.0, 0.0).astype(BF16)
    a = a[:QB]
    ahead = (col[:QB] - (a % 8 // 2 * 8 + a // 8 * 2 + a % 2)).astype(F32)
    wq = jnp.concatenate([wq_ref[0], wq_ref[1]], axis=1)
    xs, qs = [[], []], [[], []]
    for si in range(2):
        rows = jnp.concatenate([packed(pack_ref, si, PQ_AT + p * 16) for p in range(GROUP)], axis=1)
        raw = split2(mm(rows, wq))
        both = mm(pick, rows)
        start = pack_ref[0, 0, si, START_AT:START_AT + 16, :].astype(F32)[0:1, 0:1]
        live = ahead <= start
        for gg in range(2):
            g = gp * 2 + gg
            ks = [packed(pack_ref, si, pl.multiple_of(g * 64 + p * 16, 16)) for p in range(4)]
            mean = wk_ref[gg, 2 * HD:, :]
            proj_k = mm(jnp.concatenate(ks[:2], axis=1), wk_ref[gg, :2 * HD, :])
            proj_k = proj_k + mm(jnp.concatenate(ks[2:], axis=1), jnp.concatenate([mean, mean], axis=0))
            xs[gg].append(both[gg * QB:(gg + 1) * QB])
            mine, lanes = pick[gg * QB:(gg + 1) * QB], slice(gg * HD, (gg + 1) * HD)
            proj_q = mm(mine, raw[0][:, lanes]) + mm(mine, raw[1][:, lanes])
            qs[gg].append(proj_q)
            proj_k = split2(proj_k)
            kh_ref[gg, si * CB:(si + 1) * CB, :] = proj_k[0]
            kl_ref[gg, si * CB:(si + 1) * CB, :] = proj_k[1]
            logits = mm3(split2(proj_q), proj_k, NT) * SCALE
            masked = jnp.where(live, logits, NEG)
            top = masked.max(axis=1, keepdims=True)
            ex = jnp.where(live, jnp.exp(masked - top), 0.0)
            total = ex.sum(axis=1, keepdims=True)
            gate_ref[gg, si * QB:(si + 1) * QB, :] = ex / total
            if si == 0:
                log_ref[gg] = jnp.where(live, masked - top - jnp.log(total), 0.0)
    for gg in range(2):
        hi, lo = split2(jnp.concatenate(xs[gg], axis=0).T)
        xh_ref[gg] = hi
        xl_ref[gg] = lo
        hi, lo = split2(jnp.concatenate(qs[gg], axis=0).T)
        qh_ref[gg] = hi
        ql_ref[gg] = lo


def pair_spec(shape):
    return pl.BlockSpec((2,) + tuple(shape[1:]), lambda g: (g,) + (0,) * (len(shape) - 1))


def whole_spec(shape):
    return pl.BlockSpec(tuple(shape), lambda g: (0,) * len(shape))


def gate_part(at, parts, wq, wk):
    pack = (4, 4, 2, PACK, HD)
    shapes = [(2 * QB, CB), (QB, CB)] + [(GROUP * HD, 2 * QB)] * 2 + [(2 * CB, HD)] * 2 + [(HD, 2 * QB)] * 2
    shapes = [(4,) + s for s in shapes]
    return pl.pallas_call(
        gate_kernel,
        grid=(2,),
        in_specs=[pl.BlockSpec(memory_space=pltpu.SMEM)]
        + [whole_spec(v.shape) for v in parts]
        + [pair_spec(wq.shape), pair_spec(wk.shape)],
        out_specs=[whole_spec(pack)] + [pair_spec(s) for s in shapes],
        out_shape=[jax.ShapeDtypeStruct(pack, BF16)]
        + [jax.ShapeDtypeStruct(s, F32 if i < 2 else BF16) for i, s in enumerate(shapes)],
        compiler_params=pltpu.CompilerParams(vmem_limit_bytes=VMEM),
        cost_estimate=pl.CostEstimate(flops=10 ** 10, bytes_accessed=10 ** 7, transcendentals=10 ** 6),
        name="gate",
    )(at, *parts, wq, wk)


def grads_kernel(y_ref, pack_ref, t_ref, gate_ref, log_ref, xh_ref, xl_ref, kh_ref, kl_ref, qh_ref, ql_ref, g_ref, loss_ref):
    gp = pl.program_id(0)
    wide = GROUP * HD
    for gg in range(2):
        g = gp * 2 + gg
        d_q, d_k = [], []
        for si in range(2):
            yy = y_ref[0] ^ si
            teacher = jnp.concatenate(
                [
                    jnp.concatenate([t_ref[z, x, yy, 0, :, gg * 64:gg * 64 + 64] for z in range(4)], axis=1)
                    for x in range(4)
                ],
                axis=0,
            )
            target = teacher / teacher.sum(axis=1, keepdims=True)
            at = slice(si * QB, (si + 1) * QB)
            if si == 0:
                some = target > 0.0
                term = jnp.where(some, target * jnp.log(jnp.where(some, target, 1.0)), 0.0)
                term = term - target * log_ref[gg]
                loss = term.sum(axis=1, keepdims=True).sum(axis=0, keepdims=True) * (1.0 / QB)
                loss_ref[0, gg:gg + 1, :] = jnp.broadcast_to(loss, (1, 128))
            slope = split2((gate_ref[gg, at, :] - target) * (SCALE / QB))
            ks = slice(si * CB, (si + 1) * CB)
            d_q.append(mm3(slope, (kh_ref[gg, ks, :], kl_ref[gg, ks, :])))
            d_k.append(mm3((qh_ref[gg, :, at], ql_ref[gg, :, at]), slope))
        d_q = split2(jnp.concatenate(d_q, axis=0))
        g_ref[gg, :wide, :] = mm3((xh_ref[gg], xl_ref[gg]), d_q)
        d_k = jnp.concatenate(split2(jnp.concatenate(d_k, axis=1)), axis=0)
        rows = [
            jnp.concatenate([packed(pack_ref, si, pl.multiple_of(g * 64 + p * 16, 16)) for si in range(2)], axis=0)
            for p in range(4)
        ]
        ends = mm(d_k, jnp.concatenate(rows[:2], axis=1))
        mean = mm(d_k, jnp.concatenate(rows[2:], axis=1))
        ends = ends[:HD] + ends[HD:]
        mean = mean[:HD, :HD] + (mean[HD:, :HD] + mean[:HD, HD:])
        g_ref[gg, wide:wide + HD, :] = ends[:, :HD].T
        g_ref[gg, wide + HD:wide + 2 * HD, :] = ends[:, HD:].T
        g_ref[gg, wide + 2 * HD:, :] = mean.T


def gradients(y, pack, teachers, parts):
    out = (4, (GROUP + 3) * HD, HD)
    return pl.pallas_call(
        grads_kernel,
        grid=(2,),
        in_specs=[
            pl.BlockSpec(memory_space=pltpu.SMEM),
            whole_spec(pack.shape),
            pl.BlockSpec((4, 4, 2, 1, 8, 128), lambda g: (0, 0, 0, g, 0, 0)),
        ]
        + [pair_spec(v.shape) for v in parts],
        out_specs=[pair_spec(out), pl.BlockSpec((1, 2, 128), lambda g: (g, 0, 0))],
        out_shape=[jax.ShapeDtypeStruct(out, F32), jax.ShapeDtypeStruct((2, 2, 128), F32)],
        compiler_params=pltpu.CompilerParams(vmem_limit_bytes=VMEM),
        name="gradients",
    )(y, pack, teachers, *parts)


def add_kernel(a_ref, b_ref, q_ref, k_ref):
    wide = q_ref.shape[1]
    q_ref[...] = a_ref[:, :wide] + b_ref[:, :wide]
    k_ref[...] = a_ref[:, wide:] + b_ref[:, wide:]


def add_cores(a, b):
    wide = GROUP * HD
    shapes = [(4, wide, HD), (4, a.shape[1] - wide, HD)]
    return pl.pallas_call(
        add_kernel,
        grid=(2,),
        in_specs=[pair_spec(a.shape)] * 2,
        out_specs=[pair_spec(s) for s in shapes],
        out_shape=[jax.ShapeDtypeStruct(s, F32) for s in shapes],
        compiler_params=pltpu.CompilerParams(vmem_limit_bytes=VMEM),
        name="add_cores",
    )(a, b)


def shift(x, axis, by):
    return lax.ppermute(x, axis, [(i, (i + by) % 4) for i in range(4)])


def swap(x, axis):
    return lax.ppermute(x, axis, [(0, 1), (1, 0)])


def ring(v, axis):
    return [v, shift(v, axis, 1), shift(v, axis, -1), shift(v, axis, 2)]


def upward(parts):
    return [parts[0], parts[2], parts[3], parts[1]]


def per_device(queries, keys, start_block, lengths, gate_query, gate_key):
    del lengths
    z, x, y = lax.axis_index("z"), lax.axis_index("x"), lax.axis_index("y")
    q, k = queries[0], keys[0]
    start = start_block[0]
    half_q, half_k = 2 * GROUP * HD, 2 * HD
    q_parts = ring(q, "z")
    k_before, k_after = shift(k, "x", 1), shift(k, "x", -1)
    pack = pool(start_block, q, k)
    pack = ring(jnp.stack([pack, swap(pack, "y")]), "x")
    offs = (0, 3, 1, 2)
    q_pos = [start + (i * 4 + x) * 2 for i in range(4)]
    k_pos = [(z * 4 + ((x + o) & 3)) * 16 for o in offs]
    ints = lambda *v: jnp.stack([jnp.asarray(i, jnp.int32) for i in v])
    q_at = [((z + o) & 3) * 128 for o in offs]
    pos = ints(*q_pos, *k_pos, *q_at)
    bm0, ml, qs = block_scores(pos, q_parts, [k], (0,))
    pack, bm0, k_last = lax.optimization_barrier((pack, bm0, k))
    k_far = shift(k_last, "x", 2)
    packs = upward(ring(jnp.stack(upward(pack)), "z"))
    bm1, ml = block_scores(pos, [qs], [k_before, k_after], (1, 2), [ml])
    bm2, ml = block_scores(pos, [qs], [k_far], (3,), [ml])
    mls = ring(ml, "z")
    packs, _ = lax.optimization_barrier((packs, ml))
    pack, *parts = gate_part(ints(z, x), packs, gate_query, gate_key)
    parts, mls = lax.optimization_barrier((parts, mls))
    teachers = teacher_blocks(ints(x), [bm0, bm1, bm2], mls, 32)
    teachers = lax.all_to_all(teachers, ("z", "x", "y"), 0, 0, tiled=True).reshape(4, 4, 2, 2, 8, 128)
    grads, loss = gradients(ints(y), pack, teachers, parts)
    grad_q, grad_k = add_cores(grads, swap(grads, "c"))
    return grad_q, grad_k, loss[:, :, 0].reshape(1, 4)


def solution(mesh):
    fine = Mesh(mesh.devices.reshape(4, 4, 2, 2, 2), ("z", "x", "h", "y", "c"))
    ctx, dp = ("z", "x"), ("y", "c")
    placed = (
        P(dp, ctx, "h"),
        P(dp, ctx, "h"),
        P(dp),
        P(dp),
        P("h", None, None),
        P("h", None, None),
    )
    return jax.shard_map(
        per_device,
        mesh=fine,
        in_specs=placed,
        out_specs=(P("h", None, None), P("h", None, None), P(dp, "h")),
        check_vma=False,
    )
```

profile of v0, /device:TPU:1, one launch (start us, length us, event | category | flops | bytes accessed | tf_op | source)
XLA Modules:
  0.0 226.7 jit_solution(1202325322109287830)
XLA Ops:
  0.6 0.0 copy-start
  0.6 2.5 %collective-permute-start.4 = (bf16[128,2560]{1,0:T(8,128)(2,1)}, bf16[128,2560]{1,0:T(8,128)(2,1)S(1)}, u32[]{:S(2)}, u32[]{:S(2)}) collective-permute-start(bf16[128,2560]{1,0:T(8,128)(2,1)} %bitcast.34), channel_id=1, source_target_pairs={{0,32},{32,64},{64,96},{96,0},{1,33},{33,65},{65,97},{97,1},{2,34}... | collective-permute-start | bytes 1966088 | tf_op jit(solution)/shard_map/ppermute | solution.py:435
  3.2 2.2 collective-permute-start.5
  5.4 1.2 collective-permute-start.11
  6.6 1.2 collective-permute-start.6
  8.5 2.8 %pool.1 = bf16[352,128]{1,0:T(8,128)(2,1)} custom-call(s32[1]{0:T(128)} %copy.8.start_ref, bf16[128,2560]{1,0:T(8,128)(2,1)} %bitcast.37, bf16[1024,512]{1,0:T(8,128)(2,1)} %bitcast.30), custom_call_target="tpu_custom_call" | custom-call | tf_op jit(solution)/shard_map/pool/pallas_call | solution.py:209
  11.2 1.3 collective-permute-start
  12.5 2.6 %collective-permute-done = bf16[352,128]{1,0:T(8,128)(2,1)S(1)} collective-permute-done((bf16[352,128]{1,0:T(8,128)(2,1)}, bf16[352,128]{1,0:T(8,128)(2,1)S(1)}, u32[]{:S(2)}, u32[]{:S(2)}) %collective-permute-start) | collective-permute-done | bytes 90144 | tf_op jit(solution)/shard_map/ppermute | solution.py:439
  15.1 0.9 pad_maximum_fusion.1
  16.0 1.3 collective-permute-start.1
  17.3 2.7 %collective-permute-done.4.refs_1_ = bf16[128,2560]{1,0:T(8,128)(2,1)S(1)} collective-permute-done((bf16[128,2560]{1,0:T(8,128)(2,1)}, bf16[128,2560]{1,0:T(8,128)(2,1)S(1)}, u32[]{:S(2)}, u32[]{:S(2)}) %collective-permute-start.4) | collective-permute-done | bytes 655392 | tf_op jit(solution)/shard_map/ppermute | solution.py:435
  20.0 2.5 %collective-permute-start.2 = (bf16[2,352,128]{2,1,0:T(8,128)(2,1)S(1)}, bf16[2,352,128]{2,1,0:T(8,128)(2,1)}, u32[]{:S(2)}, u32[]{:S(2)}) collective-permute-start(bf16[2,352,128]{2,1,0:T(8,128)(2,1)S(1)} %pad_maximum_fusion.1), channel_id=1, source_target_pairs={{0,24},{8,0},{16,8},{24,16},{1,25},{9,1},{17,9},{25,17},{2,26},{10... | collective-permute-start | bytes 540680 | tf_op jit(solution)/shard_map/ppermute | solution.py:435
  22.5 0.0 collective-permute-done.5.refs_2_
  22.5 0.8 copy-done.9
  23.3 1.1 collective-permute-start.3
  24.4 0.6 stack.95.pos_ref
  25.0 10.0 %collective-permute-done.6.refs_3_ = bf16[128,2560]{1,0:T(8,128)(2,1)} collective-permute-done((bf16[128,2560]{1,0:T(8,128)(2,1)}, bf16[128,2560]{1,0:T(8,128)(2,1)}, u32[]{:S(2)}, u32[]{:S(2)}) %collective-permute-start.6) | collective-permute-done | bytes 655392 | tf_op jit(solution)/shard_map/ppermute | solution.py:435
  35.0 2.5 %collective-permute-start.12 = (bf16[1024,512]{1,0:T(8,128)(2,1)S(1)}, bf16[1024,512]{1,0:T(8,128)(2,1)S(1)}, u32[]{:S(2)}, u32[]{:S(2)}) collective-permute-start(bf16[1024,512]{1,0:T(8,128)(2,1)S(1)} %bitcast.32), channel_id=1, source_target_pairs={{0,24},{8,0},{16,8},{24,16},{1,25},{9,1},{17,9},{25,17},{2,26},{10... | collective-permute-start | bytes 3145736 | tf_op jit(solution)/shard_map/ppermute | solution.py:435
  37.5 30.9 %block_scores.3 = (f32[4,5,16,512]{3,2,1,0:T(8,128)}, f32[4,5,2,512]{3,2,1,0:T(2,128)}, bf16[4,5,512,256]{3,2,1,0:T(8,128)(2,1)}) custom-call(s32[12]{0:T(128)} %stack.95.pos_ref, bf16[128,2560]{1,0:T(8,128)(2,1)} %bitcast.38, bf16[128,2560]{1,0:T(8,128)(2,1)} %copy-done.8, bf16[128,2560]{1,0:T(8,128)(2,1)} %copy-done.9, ...), custom_call_target="tpu_custom_call" | custom-call | tf_op jit(solution)/shard_map/block_scores/pallas_call | solution.py:171
  68.4 0.0 collective-permute-done.1
  68.4 0.0 collective-permute-done.2
  68.4 0.0 collective-permute-done.3
  68.4 0.1 collective-permute-start.10
  68.5 1.1 pad_maximum_fusion.refs_0_
  69.6 0.0 copy-start.7
  69.6 0.1 collective-permute-start.7
  69.7 0.1 collective-permute-start.8
  69.8 0.0 collective-permute-done.11.refs_1_
  69.8 0.0 copy-start.5
  69.8 1.6 collective-permute-start.9
  71.4 0.6 pad_add_fusion.at_ref
  72.1 0.0 collective-permute-done.12.refs_2_
  72.1 1.1 copy-done.6
  73.1 50.5 %block_scores.4 = (f32[4,5,32,512]{3,2,1,0:T(8,128)}, f32[4,5,2,512]{3,2,1,0:T(2,128)}) custom-call(s32[12]{0:T(128)} %stack.95.pos_ref, bf16[4,5,512,256]{3,2,1,0:T(8,128)(2,1)} %get-tuple-element.50.refs_0_, bf16[1024,512]{1,0:T(8,128)(2,1)} %copy-done.5, bf16[1024,512]{1,0:T(8,128)(2,1)} %copy-done.6, f32[4,5,2,512]{3,2,1,0:T(2,128)} %get-tuple-element.52.refs_3_), custom_call_target="tpu_custom_call" | custom-call | tf_op jit(solution)/shard_map/block_scores/pallas_call | solution.py:171
  123.6 0.0 collective-permute-done.10.refs_1_
  123.6 1.0 copy-done.3
  124.6 11.8 %block_scores.5 = (f32[4,5,16,512]{3,2,1,0:T(8,128)}, f32[4,5,2,512]{3,2,1,0:T(2,128)}) custom-call(s32[12]{0:T(128)} %stack.95.pos_ref, bf16[4,5,512,256]{3,2,1,0:T(8,128)(2,1)} %get-tuple-element.50.refs_0_, bf16[1024,512]{1,0:T(8,128)(2,1)} %copy-done.3, f32[4,5,2,512]{3,2,1,0:T(2,128)} %get-tuple-element.53.refs_2_), custom_call_target="tpu_custom_call" | custom-call | tf_op jit(solution)/shard_map/block_scores/pallas_call | solution.py:171
  136.4 0.0 collective-permute-start.13
  136.4 2.7 %collective-permute-start.14 = (f32[4,5,2,512]{3,2,1,0:T(2,128)}, f32[4,5,2,512]{3,2,1,0:T(2,128)S(1)}, u32[]{:S(2)}, u32[]{:S(2)}) collective-permute-start(f32[4,5,2,512]{3,2,1,0:T(2,128)} %get-tuple-element.71.refs_3_), channel_id=1, source_target_pairs={{0,96},{32,0},{64,32},{96,64},{1,97},{33,1},{65,33},{97,65},{2,98}... | collective-permute-start | bytes 245768 | tf_op jit(solution)/shard_map/ppermute | solution.py:435
  139.1 0.0 collective-permute-done.7.refs_1_
  139.1 0.0 collective-permute-start.15
  139.1 0.0 collective-permute-done.8.refs_2_
  139.1 0.0 collective-permute-done.9.refs_3_
  139.1 0.9 copy-done.13
  140.0 0.2 copy-done.14
  140.3 0.9 copy-done.15
  141.1 7.3 %gate.1 = (bf16[4,4,2,352,128]{4,3,2,1,0:T(8,128)(2,1)}, f32[4,64,256]{2,1,0:T(8,128)}, f32[4,32,256]{2,1,0:T(8,128)}, bf16[4,640,64]{2,1,0:T(8,128)(2,1)}, bf16...) custom-call(s32[2]{0:T(128)} %pad_add_fusion.at_ref, ...), custom_call_target="tpu_custom_call" | custom-call | flops 10000000000 | bytes 10000000 | tf_op jit(solution)/shard_map/gate/pallas_call | solution.py:338
  148.4 0.0 collective-permute-done.13.refs_4_
  148.4 0.0 collective-permute-done.14.refs_5_
  148.5 0.0 collective-permute-done.15.refs_6_
  148.5 0.6 copy-done.10
  149.0 0.0 copy-done.11
  149.1 0.0 copy-done.12
  149.1 3.6 %teacher.1 = f32[32,2,8,128]{3,2,1,0:T(8,128)} custom-call(s32[1]{0:T(128)} %bitcast.2.x_ref, f32[4,5,16,512]{3,2,1,0:T(8,128)} %get-tuple-element.60.refs_0_, f32[4,5,32,512]{3,2,1,0:T(8,128)} %get-tuple-element.61.refs_1_, f32[4,5,16,512]{3,2,1,0:T(8,128)} %get-tuple-element.62.refs_2_, f32[4,5,2,512]{3,2,1,0:T(2,128)} %get-tuple-element.71.refs_3_, ...), custom_call_target="tpu_custom_call" | custom-call | tf_op jit(solution)/shard_map/teacher/pallas_call | solution.py:249
  152.7 26.3 %all-to-all-start = ((f32[32,2,8,128]{3,2,1,0:T(8,128)}), f32[32,2,8,128]{3,2,1,0:T(8,128)S(1)}, u32[]{:S(2)}, u32[]{:S(2)}) async-start(f32[32,2,8,128]{3,2,1,0:T(8,128)} %teacher.1), calls=%async_computation | async-start | bytes 524288 | tf_op jit(solution)/shard_map/all_to_all | solution.py:477
  179.0 8.3 %all-to-all-done = f32[32,2,8,128]{3,2,1,0:T(8,128)S(1)} async-done(((f32[32,2,8,128]{3,2,1,0:T(8,128)}), f32[32,2,8,128]{3,2,1,0:T(8,128)S(1)}, u32[]{:S(2)}, u32[]{:S(2)}) %all-to-all-start) | async-done | bytes 262176 | tf_op jit(solution)/shard_map/all_to_all | solution.py:477
  187.3 0.7 copy-done.4
  188.0 6.5 %gradients.1 = (f32[4,1024,128]{2,1,0:T(8,128)}, f32[2,2,128]{2,1,0:T(2,128)}) custom-call(s32[1]{0:T(128)} %bitcast.y_ref, bf16[4,4,2,352,128]{4,3,2,1,0:T(8,128)(2,1)} %get-tuple-element.59.pack_ref, f32[4,4,2,2,8,128]{5,4,3,2,1,0:T(8,128)} %bitcast.39, f32[4,64,256]{2,1,0:T(8,128)} %get-tuple-element.75.gate_ref, ...), custom_call_target="tpu_custom_call" | custom-call | tf_op jit(solution)/shard_map/gradients/pallas_call | solution.py:398
  194.5 23.6 %collective-permute-start.16 = (f32[4,1024,128]{2,1,0:T(8,128)}, f32[4,1024,128]{2,1,0:T(8,128)S(1)}, u32[]{:S(2)}, u32[]{:S(2)}) collective-permute-start(f32[4,1024,128]{2,1,0:T(8,128)} %get-tuple-element.83.a_ref), channel_id=1, source_target_pairs={{0,1},{1,0},{2,3},{3,2},{4,5},{5,4},{6,7},{7,6},{8,9},{9,8},{10,11... | collective-permute-start | bytes 6291464 | tf_op jit(solution)/shard_map/ppermute | solution.py:439
  218.1 0.8 slice_reduce_fusion
  218.9 0.6 reshape_squeeze.3
  219.5 2.6 %collective-permute-done.16.b_ref = f32[4,1024,128]{2,1,0:T(8,128)S(1)} collective-permute-done((f32[4,1024,128]{2,1,0:T(8,128)}, f32[4,1024,128]{2,1,0:T(8,128)S(1)}, u32[]{:S(2)}, u32[]{:S(2)}) %collective-permute-start.16) | collective-permute-done | bytes 2097184 | tf_op jit(solution)/shard_map/ppermute | solution.py:439
  222.1 1.4 copy-done.2
  223.5 3.2 %add_cores.1 = (f32[4,640,128]{2,1,0:T(8,128)}, f32[4,384,128]{2,1,0:T(8,128)}) custom-call(f32[4,1024,128]{2,1,0:T(8,128)} %get-tuple-element.83.a_ref, f32[4,1024,128]{2,1,0:T(8,128)} %copy-done.2), custom_call_target="tpu_custom_call" | custom-call | tf_op jit(solution)/shard_map/add_cores/pallas_call | solution.py:423
  (18 shorter events, 0.0 us)
Async XLA Ops:
  0.6 34.3 %copy-start = (bf16[1,1024,512]{2,1,0:T(8,128)(2,1)S(1)}, bf16[1,1024,512]{2,1,0:T(8,128)(2,1)}, u32[]{:S(2)}) copy-start(bf16[1,1024,512]{2,1,0:T(8,128)(2,1)} %param.7) | copy-start | bytes 3145732
  0.6 19.3 %collective-permute-start.4 = (bf16[128,2560]{1,0:T(8,128)(2,1)}, bf16[128,2560]{1,0:T(8,128)(2,1)S(1)}, u32[]{:S(2)}, u32[]{:S(2)}) collective-permute-start(bf16[128,2560]{1,0:T(8,128)(2,1)} %bitcast.34), channel_id=1, source_target_pairs={{0,32},{32,64},{64,96},{96,0},{1,33},{33,65},{65,97},{97,1},{2,34}... | collective-permute-start | bytes 1966088 | tf_op jit(solution)/shard_map/ppermute | solution.py:435
  3.2 19.3 %collective-permute-start.5 = (bf16[128,2560]{1,0:T(8,128)(2,1)}, bf16[128,2560]{1,0:T(8,128)(2,1)S(1)}, u32[]{:S(2)}, u32[]{:S(2)}) collective-permute-start(bf16[128,2560]{1,0:T(8,128)(2,1)} %bitcast.35), channel_id=1, source_target_pairs={{0,96},{32,0},{64,32},{96,64},{1,97},{33,1},{65,33},{97,65},{2,98}... | collective-permute-start | bytes 1966088 | tf_op jit(solution)/shard_map/ppermute | solution.py:435
  5.4 64.4 %collective-permute-start.11 = (bf16[1024,512]{1,0:T(8,128)(2,1)}, bf16[1024,512]{1,0:T(8,128)(2,1)S(1)}, u32[]{:S(2)}, u32[]{:S(2)}) collective-permute-start(bf16[1024,512]{1,0:T(8,128)(2,1)} %bitcast.29), channel_id=1, source_target_pairs={{0,8},{8,16},{16,24},{24,0},{1,9},{9,17},{17,25},{25,1},{2,10},{10... | collective-permute-start | bytes 3145736 | tf_op jit(solution)/shard_map/ppermute | solution.py:435
  6.6 28.4 %collective-permute-start.6 = (bf16[128,2560]{1,0:T(8,128)(2,1)}, bf16[128,2560]{1,0:T(8,128)(2,1)}, u32[]{:S(2)}, u32[]{:S(2)}) collective-permute-start(bf16[128,2560]{1,0:T(8,128)(2,1)} %bitcast.36), channel_id=1, source_target_pairs={{0,64},{32,96},{64,0},{96,32},{1,65},{33,97},{65,1},{97,33},{2,66}... | collective-permute-start | bytes 1966088 | tf_op jit(solution)/shard_map/ppermute | solution.py:435
  11.2 57.2 %copy-start.1 = (bf16[1,1024,512]{2,1,0:T(8,128)(2,1)S(1)}, bf16[1,1024,512]{2,1,0:T(8,128)(2,1)}, u32[]{:S(2)}) copy-start(bf16[1,1024,512]{2,1,0:T(8,128)(2,1)} %param.7) | copy-start | bytes 3145732
  11.2 3.9 %collective-permute-start = (bf16[352,128]{1,0:T(8,128)(2,1)}, bf16[352,128]{1,0:T(8,128)(2,1)S(1)}, u32[]{:S(2)}, u32[]{:S(2)}) collective-permute-start(bf16[352,128]{1,0:T(8,128)(2,1)} %pool.1), channel_id=1, source_target_pairs={{0,2},{2,0},{1,3},{3,1},{4,6},{6,4},{5,7},{7,5},{8,10},{10,8},{9,1... | collective-permute-start | bytes 270344 | tf_op jit(solution)/shard_map/ppermute | solution.py:439
  16.0 52.4 %collective-permute-start.1 = (bf16[2,352,128]{2,1,0:T(8,128)(2,1)S(1)}, bf16[2,352,128]{2,1,0:T(8,128)(2,1)S(1)}, u32[]{:S(2)}, u32[]{:S(2)}) collective-permute-start(bf16[2,352,128]{2,1,0:T(8,128)(2,1)S(1)} %pad_maximum_fusion.1), channel_id=1, source_target_pairs={{0,8},{8,16},{16,24},{24,0},{1,9},{9,17},{17,25},{25,1},{2,10},{10... | collective-permute-start | bytes 540680 | tf_op jit(solution)/shard_map/ppermute | solution.py:435
  20.0 2.5 %copy-start.8 = (bf16[128,2560]{1,0:T(8,128)(2,1)}, bf16[128,2560]{1,0:T(8,128)(2,1)S(1)}, u32[]{:S(2)}) copy-start(bf16[128,2560]{1,0:T(8,128)(2,1)S(1)} %collective-permute-done.4.refs_1_) | copy-start | bytes 1966084
  20.0 48.4 %collective-permute-start.2 = (bf16[2,352,128]{2,1,0:T(8,128)(2,1)S(1)}, bf16[2,352,128]{2,1,0:T(8,128)(2,1)}, u32[]{:S(2)}, u32[]{:S(2)}) collective-permute-start(bf16[2,352,128]{2,1,0:T(8,128)(2,1)S(1)} %pad_maximum_fusion.1), channel_id=1, source_target_pairs={{0,24},{8,0},{16,8},{24,16},{1,25},{9,1},{17,9},{25,17},{2,26},{10... | collective-permute-start | bytes 540680 | tf_op jit(solution)/shard_map/ppermute | solution.py:435
  22.5 0.8 copy-start.9
  23.3 45.1 %collective-permute-start.3 = (bf16[2,352,128]{2,1,0:T(8,128)(2,1)S(1)}, bf16[2,352,128]{2,1,0:T(8,128)(2,1)}, u32[]{:S(2)}, u32[]{:S(2)}) collective-permute-start(bf16[2,352,128]{2,1,0:T(8,128)(2,1)S(1)} %pad_maximum_fusion.1), channel_id=1, source_target_pairs={{0,16},{8,24},{16,0},{24,8},{1,17},{9,25},{17,1},{25,9},{2,18},{10... | collective-permute-start | bytes 540680 | tf_op jit(solution)/shard_map/ppermute | solution.py:435
  35.0 37.1 %collective-permute-start.12 = (bf16[1024,512]{1,0:T(8,128)(2,1)S(1)}, bf16[1024,512]{1,0:T(8,128)(2,1)S(1)}, u32[]{:S(2)}, u32[]{:S(2)}) collective-permute-start(bf16[1024,512]{1,0:T(8,128)(2,1)S(1)} %bitcast.32), channel_id=1, source_target_pairs={{0,24},{8,0},{16,8},{24,16},{1,25},{9,1},{17,9},{25,17},{2,26},{10... | collective-permute-start | bytes 3145736 | tf_op jit(solution)/shard_map/ppermute | solution.py:435
  68.4 55.2 %collective-permute-start.10 = (bf16[1024,512]{1,0:T(8,128)(2,1)S(1)}, bf16[1024,512]{1,0:T(8,128)(2,1)S(1)}, u32[]{:S(2)}, u32[]{:S(2)}) collective-permute-start(bf16[1024,512]{1,0:T(8,128)(2,1)S(1)} %bitcast.33), channel_id=1, source_target_pairs={{0,16},{8,24},{16,0},{24,8},{1,17},{9,25},{17,1},{25,9},{2,18},{10... | collective-permute-start | bytes 3145736 | tf_op jit(solution)/shard_map/ppermute | solution.py:435
  69.6 66.8 %copy-start.7 = (bf16[4,2,352,128]{3,2,1,0:T(8,128)(2,1)}, bf16[4,2,352,128]{3,2,1,0:T(8,128)(2,1)S(1)}, u32[]{:S(2)}) copy-start(bf16[4,2,352,128]{3,2,1,0:T(8,128)(2,1)S(1)} %pad_maximum_fusion.refs_0_) | copy-start | bytes 2162692
  69.6 69.5 %collective-permute-start.7 = (bf16[4,2,352,128]{3,2,1,0:T(8,128)(2,1)S(1)}, bf16[4,2,352,128]{3,2,1,0:T(8,128)(2,1)S(1)}, u32[]{:S(2)}, u32[]{:S(2)}) collective-permute-start(bf16[4,2,352,128]{3,2,1,0:T(8,128)(2,1)S(1)} %pad_maximum_fusion.refs_0_), channel_id=1, source_target_pairs={{0,96},{32,0},{64,32},{96,64},{1,97},{33,1},{65,33},{97,65},{2,98}... | collective-permute-start | bytes 2162696 | tf_op jit(solution)/shard_map/ppermute | solution.py:435
  69.7 69.4 %collective-permute-start.8 = (bf16[4,2,352,128]{3,2,1,0:T(8,128)(2,1)S(1)}, bf16[4,2,352,128]{3,2,1,0:T(8,128)(2,1)S(1)}, u32[]{:S(2)}, u32[]{:S(2)}) collective-permute-start(bf16[4,2,352,128]{3,2,1,0:T(8,128)(2,1)S(1)} %pad_maximum_fusion.refs_0_), channel_id=1, source_target_pairs={{0,64},{32,96},{64,0},{96,32},{1,65},{33,97},{65,1},{97,33},{2,66}... | collective-permute-start | bytes 2162696 | tf_op jit(solution)/shard_map/ppermute | solution.py:435
  69.8 2.3 copy-start.5
  69.8 69.3 %collective-permute-start.9 = (bf16[4,2,352,128]{3,2,1,0:T(8,128)(2,1)S(1)}, bf16[4,2,352,128]{3,2,1,0:T(8,128)(2,1)S(1)}, u32[]{:S(2)}, u32[]{:S(2)}) collective-permute-start(bf16[4,2,352,128]{3,2,1,0:T(8,128)(2,1)S(1)} %pad_maximum_fusion.refs_0_), channel_id=1, source_target_pairs={{0,32},{32,64},{64,96},{96,0},{1,33},{33,65},{65,97},{97,1},{2,34}... | collective-permute-start | bytes 2162696 | tf_op jit(solution)/shard_map/ppermute | solution.py:435
  72.1 1.1 copy-start.6
  123.6 1.0 copy-start.3
  136.4 12.0 %collective-permute-start.13 = (f32[4,5,2,512]{3,2,1,0:T(2,128)}, f32[4,5,2,512]{3,2,1,0:T(2,128)S(1)}, u32[]{:S(2)}, u32[]{:S(2)}) collective-permute-start(f32[4,5,2,512]{3,2,1,0:T(2,128)} %get-tuple-element.71.refs_3_), channel_id=1, source_target_pairs={{0,32},{32,64},{64,96},{96,0},{1,33},{33,65},{65,97},{97,1},{2,34}... | collective-permute-start | bytes 245768 | tf_op jit(solution)/shard_map/ppermute | solution.py:435
  136.4 12.0 %collective-permute-start.14 = (f32[4,5,2,512]{3,2,1,0:T(2,128)}, f32[4,5,2,512]{3,2,1,0:T(2,128)S(1)}, u32[]{:S(2)}, u32[]{:S(2)}) collective-permute-start(f32[4,5,2,512]{3,2,1,0:T(2,128)} %get-tuple-element.71.refs_3_), channel_id=1, source_target_pairs={{0,96},{32,0},{64,32},{96,64},{1,97},{33,1},{65,33},{97,65},{2,98}... | collective-permute-start | bytes 245768 | tf_op jit(solution)/shard_map/ppermute | solution.py:435
  139.1 0.9 copy-start.13
  139.1 9.4 %collective-permute-start.15 = (f32[4,5,2,512]{3,2,1,0:T(2,128)}, f32[4,5,2,512]{3,2,1,0:T(2,128)S(1)}, u32[]{:S(2)}, u32[]{:S(2)}) collective-permute-start(f32[4,5,2,512]{3,2,1,0:T(2,128)} %get-tuple-element.71.refs_3_), channel_id=1, source_target_pairs={{0,64},{32,96},{64,0},{96,32},{1,65},{33,97},{65,1},{97,33},{2,66}... | collective-permute-start | bytes 245768 | tf_op jit(solution)/shard_map/ppermute | solution.py:435
  139.1 1.2 copy-start.14
  140.3 0.9 copy-start.15
  148.4 0.6 copy-start.10
  148.4 0.7 copy-start.11
  148.5 0.7 copy-start.12
  152.7 34.5 %all-to-all-start = ((f32[32,2,8,128]{3,2,1,0:T(8,128)}), f32[32,2,8,128]{3,2,1,0:T(8,128)S(1)}, u32[]{:S(2)}, u32[]{:S(2)}) async-start(f32[32,2,8,128]{3,2,1,0:T(8,128)} %teacher.1), calls=%async_computation | async-start | bytes 524288 | tf_op jit(solution)/shard_map/all_to_all | solution.py:477
  187.3 0.7 copy-start.4
  194.5 27.6 %collective-permute-start.16 = (f32[4,1024,128]{2,1,0:T(8,128)}, f32[4,1024,128]{2,1,0:T(8,128)S(1)}, u32[]{:S(2)}, u32[]{:S(2)}) collective-permute-start(f32[4,1024,128]{2,1,0:T(8,128)} %get-tuple-element.83.a_ref), channel_id=1, source_target_pairs={{0,1},{1,0},{2,3},{3,2},{4,5},{5,4},{6,7},{7,6},{8,9},{9,8},{10,11... | collective-permute-start | bytes 6291464 | tf_op jit(solution)/shard_map/ppermute | solution.py:439
  222.1 1.4 copy-start.2
where the time goes:
time: 224 us; the launch traced here: 227 us
  Pallas kernels  117 us (52%)
  starting transfers between devices  70.2 us (31%)
  waiting for transfers between devices  26.1 us (12%)
  local copies, waits for them, and re-layouts  9.65 us (4%)
  other arithmetic  2.65 us (1%)
    pallas_call x3, Pallas kernels, block_scores(): pl.pallas_call(functools.partial(scores_kernel, n_q=len(q_parts), shards=...  93.2 us
    all_to_all x1, starting transfers between devices, per_device(): lax.all_to_all(teachers, ('z', 'x', 'y'), 0, 0, tiled=True)  26.3 us
    ppermute x2, starting transfers between devices, swap(): return lax.ppermute(x, axis, [(0, 1), (1, 0)])  24.9 us
    ppermute x15, starting transfers between devices, shift(): return lax.ppermute(x, axis, [(i, (i + by) % 4) for i in range(4)])  19 us
    ppermute x15, waiting for transfers between devices, shift(): return lax.ppermute(x, axis, [(i, (i + by) % 4) for i in range(4)])  12.6 us
    all_to_all x1, waiting for transfers between devices, per_device(): lax.all_to_all(teachers, ('z', 'x', 'y'), 0, 0, tiled=True)  8.27 us
    unnamed x32, local copies, waits for them, and re-layouts  7.66 us
    pallas_call x1, Pallas kernels, gate_part(): pl.pallas_call(gate_kernel, grid=(2,), in_specs=[pl.BlockSpec(memory_spac...  7.28 us
  transfers between devices with their start and end apart: 18, of which 5 were waited for; matrix products, arithmetic and copies ran while one was open for 2% of the time, Pallas kernels for 46%

commit v1 on v0

--- a/solution.py
+++ b/solution.py
@@ -456,6 +456,7 @@
     q_parts = ring(q, "z")
     k_before, k_after = shift(k, "x", 1), shift(k, "x", -1)
     pack = pool(start_block, q, k)
+    pack, k_before, k_after = lax.optimization_barrier((pack, k_before, k_after))
     pack = ring(jnp.stack([pack, swap(pack, "y")]), "x")
     offs = (0, 3, 1, 2)
     q_pos = [start + (i * 4 + x) * 2 for i in range(4)]

time: 224 us -> 225 us (level); the launches traced: 227 us -> 222 us
  starting transfers between devices: 70.2 us -> 64.5 us
  waiting for transfers between devices: 26.1 us -> 28.7 us
    ppermute x2, starting transfers between devices: 24.9 us -> 1.77 us  [swap(): return lax.ppermute(x, axis, [(0, 1), (1, 0)])]
    all_to_all x1, starting transfers between devices: 26.3 us -> 44.7 us  [per_device(): lax.all_to_all(teachers, ('z', 'x', 'y'), 0, 0, tiled=True)]
    unnamed x32 -> x26, local copies, waits for them, and re-layouts: 7.66 us -> 5.64 us
  transfers between devices with their start and end apart: 18 -> 18, of which waited for: 5 -> 5; matrix products, arithmetic and copies ran while one was open for 2% -> 2% of each run, Pallas kernels for 46% -> 47%
where the time goes in v1:
time: 225 us; the launch traced here: 222 us
  Pallas kernels  117 us (52%)
  starting transfers between devices  64.5 us (29%)
  waiting for transfers between devices  28.7 us (13%)
  local copies, waits for them, and re-layouts  7.61 us (3%)
  other arithmetic  2.66 us (1%)
    pallas_call x3, Pallas kernels, block_scores(): pl.pallas_call(functools.partial(scores_kernel, n_q=len(q_parts), shards=...  93.2 us
    all_to_all x1, starting transfers between devices, per_device(): lax.all_to_all(teachers, ('z', 'x', 'y'), 0, 0, tiled=True)  44.7 us
    ppermute x15, starting transfers between devices, shift(): return lax.ppermute(x, axis, [(i, (i + by) % 4) for i in range(4)])  18 us
    ppermute x15, waiting for transfers between devices, shift(): return lax.ppermute(x, axis, [(i, (i + by) % 4) for i in range(4)])  14.9 us
    all_to_all x1, waiting for transfers between devices, per_device(): lax.all_to_all(teachers, ('z', 'x', 'y'), 0, 0, tiled=True)  8.27 us
    pallas_call x1, Pallas kernels, gate_part(): pl.pallas_call(gate_kernel, grid=(2,), in_specs=[pl.BlockSpec(memory_spac...  7.33 us
    pallas_call x1, Pallas kernels, gradients(): pl.pallas_call(grads_kernel, grid=(2,), in_specs=[pl.BlockSpec(memory_spa...  6.48 us
    unnamed x26, local copies, waits for them, and re-layouts  5.64 us
  transfers between devices with their start and end apart: 18, of which 5 were waited for; matrix products, arithmetic and copies ran while one was open for 2% of the time, Pallas kernels for 47%

profile of v1, /device:TPU:1, one launch (start us, length us, event | category | flops | bytes accessed | tf_op | source)
XLA Modules:
  0.0 221.5 jit_solution(8350211356394785354)
XLA Ops:
  0.6 2.1 collective-permute-start
  2.7 1.4 collective-permute-start.1
  4.1 1.8 collective-permute-start.6
  5.8 2.1 collective-permute-start.7
  8.0 1.3 collective-permute-start.8
  9.9 2.8 %pool.1 = bf16[352,128]{1,0:T(8,128)(2,1)} custom-call(s32[1]{0:T(128)} %copy.8.start_ref, bf16[128,2560]{1,0:T(8,128)(2,1)} %bitcast.37, bf16[1024,512]{1,0:T(8,128)(2,1)} %bitcast.31), custom_call_target="tpu_custom_call" | custom-call | tf_op jit(solution)/shard_map/pool/pallas_call | solution.py:209
  12.7 14.1 %collective-permute-done.refs_1_ = bf16[1024,512]{1,0:T(8,128)(2,1)S(1)} collective-permute-done((bf16[1024,512]{1,0:T(8,128)(2,1)}, bf16[1024,512]{1,0:T(8,128)(2,1)S(1)}, u32[]{:S(2)}, u32[]{:S(2)}) %collective-permute-start) | collective-permute-done | bytes 1048608 | tf_op jit(solution)/shard_map/ppermute | solution.py:435
  26.8 0.0 collective-permute-done.1.refs_2_
  26.8 1.7 collective-permute-start.2
  28.5 2.5 %collective-permute-done.2 = bf16[352,128]{1,0:T(8,128)(2,1)S(1)} collective-permute-done((bf16[352,128]{1,0:T(8,128)(2,1)}, bf16[352,128]{1,0:T(8,128)(2,1)S(1)}, u32[]{:S(2)}, u32[]{:S(2)}) %collective-permute-start.2) | collective-permute-done | bytes 90144 | tf_op jit(solution)/shard_map/ppermute | solution.py:439
  31.0 0.9 pad_maximum_fusion.1
  31.9 1.0 collective-permute-start.3
  32.9 1.7 collective-permute-start.4
  34.6 0.0 collective-permute-done.6.refs_1_
  34.7 1.0 collective-permute-start.5
  35.7 0.6 stack.95.pos_ref
  36.3 0.0 collective-permute-done.7.refs_2_
  36.3 0.8 collective-permute-done.8.refs_3_
  37.0 30.9 %block_scores.3 = (f32[4,5,16,512]{3,2,1,0:T(8,128)}, f32[4,5,2,512]{3,2,1,0:T(2,128)}, bf16[4,5,512,256]{3,2,1,0:T(8,128)(2,1)}) custom-call(s32[12]{0:T(128)} %stack.95.pos_ref, bf16[128,2560]{1,0:T(8,128)(2,1)} %bitcast.38, bf16[128,2560]{1,0:T(8,128)(2,1)} %collective-permute-done.6.refs_1_, bf16[128,2560]{1,0:T(8,128)(2,1)} %collective-permute-done.7.refs_2_, ...), custom_call_target="tpu_custom_call" | custom-call | tf_op jit(solution)/shard_map/block_scores/pallas_call | solution.py:171
  68.0 0.0 collective-permute-done.3
  68.0 0.0 collective-permute-done.4
  68.0 0.0 collective-permute-done.5
  68.0 0.0 copy-done
  68.0 0.1 collective-permute-start.12
  68.1 1.1 pad_maximum_fusion.refs_0_
  69.2 0.0 copy-start.6
  69.2 0.1 collective-permute-start.10
  69.3 0.1 collective-permute-start.11
  69.4 2.7 %collective-permute-start.9 = (bf16[4,2,352,128]{3,2,1,0:T(8,128)(2,1)S(1)}, bf16[4,2,352,128]{3,2,1,0:T(8,128)(2,1)S(1)}, u32[]{:S(2)}, u32[]{:S(2)}) collective-permute-start(bf16[4,2,352,128]{3,2,1,0:T(8,128)(2,1)S(1)} %pad_maximum_fusion.refs_0_), channel_id=1, source_target_pairs={{0,96},{32,0},{64,32},{96,64},{1,97},{33,1},{65,33},{97,65},{2,98}... | collective-permute-start | bytes 2162696 | tf_op jit(solution)/shard_map/ppermute | solution.py:435
  72.1 0.7 pad_add_fusion.at_ref
  72.7 50.5 %block_scores.4 = (f32[4,5,32,512]{3,2,1,0:T(8,128)}, f32[4,5,2,512]{3,2,1,0:T(2,128)}) custom-call(s32[12]{0:T(128)} %stack.95.pos_ref, bf16[4,5,512,256]{3,2,1,0:T(8,128)(2,1)} %get-tuple-element.54.refs_0_, bf16[1024,512]{1,0:T(8,128)(2,1)} %copy-done.4, bf16[1024,512]{1,0:T(8,128)(2,1)} %copy-done.5, f32[4,5,2,512]{3,2,1,0:T(2,128)} %get-tuple-element.58.refs_3_), custom_call_target="tpu_custom_call" | custom-call | tf_op jit(solution)/shard_map/block_scores/pallas_call | solution.py:171
  123.2 0.0 collective-permute-done.12.refs_1_
  123.2 0.0 copy-start.2
  123.2 1.0 copy-done.2
  124.2 11.8 %block_scores.5 = (f32[4,5,16,512]{3,2,1,0:T(8,128)}, f32[4,5,2,512]{3,2,1,0:T(2,128)}) custom-call(s32[12]{0:T(128)} %stack.95.pos_ref, bf16[4,5,512,256]{3,2,1,0:T(8,128)(2,1)} %get-tuple-element.54.refs_0_, bf16[1024,512]{1,0:T(8,128)(2,1)} %copy-done.2, f32[4,5,2,512]{3,2,1,0:T(2,128)} %get-tuple-element.59.refs_2_), custom_call_target="tpu_custom_call" | custom-call | tf_op jit(solution)/shard_map/block_scores/pallas_call | solution.py:171
  136.0 0.0 collective-permute-start.13
  136.0 2.7 %collective-permute-start.14 = (f32[4,5,2,512]{3,2,1,0:T(2,128)}, f32[4,5,2,512]{3,2,1,0:T(2,128)S(1)}, u32[]{:S(2)}, u32[]{:S(2)}) collective-permute-start(f32[4,5,2,512]{3,2,1,0:T(2,128)} %get-tuple-element.77.refs_3_), channel_id=1, source_target_pairs={{0,96},{32,0},{64,32},{96,64},{1,97},{33,1},{65,33},{97,65},{2,98}... | collective-permute-start | bytes 245768 | tf_op jit(solution)/shard_map/ppermute | solution.py:435
  138.7 0.0 collective-permute-done.10.refs_2_
  138.7 0.0 collective-permute-start.15
  138.7 0.0 collective-permute-done.11.refs_3_
  138.7 0.0 copy-start.11
  138.7 0.0 collective-permute-done.9.refs_1_
  138.7 0.8 copy-done.10
  139.5 0.2 copy-done.11
  139.8 0.9 copy-done.12
  140.6 7.3 %gate.1 = (bf16[4,4,2,352,128]{4,3,2,1,0:T(8,128)(2,1)}, f32[4,64,256]{2,1,0:T(8,128)}, f32[4,32,256]{2,1,0:T(8,128)}, bf16[4,640,64]{2,1,0:T(8,128)(2,1)}, bf16...) custom-call(s32[2]{0:T(128)} %pad_add_fusion.at_ref, ...), custom_call_target="tpu_custom_call" | custom-call | flops 10000000000 | bytes 10000000 | tf_op jit(solution)/shard_map/gate/pallas_call | solution.py:338
  148.0 0.0 collective-permute-done.13.refs_4_
  148.0 0.0 collective-permute-done.14.refs_5_
  148.0 0.0 copy-start.8
  148.0 0.0 collective-permute-done.15.refs_6_
  148.0 0.6 copy-done.7
  148.6 0.0 copy-done.8
  148.6 0.1 copy-done.9
  148.7 3.6 %teacher.1 = f32[32,2,8,128]{3,2,1,0:T(8,128)} custom-call(s32[1]{0:T(128)} %bitcast.2.x_ref, f32[4,5,16,512]{3,2,1,0:T(8,128)} %get-tuple-element.66.refs_0_, f32[4,5,32,512]{3,2,1,0:T(8,128)} %get-tuple-element.67.refs_1_, f32[4,5,16,512]{3,2,1,0:T(8,128)} %get-tuple-element.68.refs_2_, f32[4,5,2,512]{3,2,1,0:T(2,128)} %get-tuple-element.77.refs_3_, ...), custom_call_target="tpu_custom_call" | custom-call | tf_op jit(solution)/shard_map/teacher/pallas_call | solution.py:249
  152.3 44.7 %all-to-all-start = ((f32[32,2,8,128]{3,2,1,0:T(8,128)}), f32[32,2,8,128]{3,2,1,0:T(8,128)S(1)}, u32[]{:S(2)}, u32[]{:S(2)}) async-start(f32[32,2,8,128]{3,2,1,0:T(8,128)} %teacher.1), calls=%async_computation | async-start | bytes 524288 | tf_op jit(solution)/shard_map/all_to_all | solution.py:478
  197.0 8.3 %all-to-all-done = f32[32,2,8,128]{3,2,1,0:T(8,128)S(1)} async-done(((f32[32,2,8,128]{3,2,1,0:T(8,128)}), f32[32,2,8,128]{3,2,1,0:T(8,128)S(1)}, u32[]{:S(2)}, u32[]{:S(2)}) %all-to-all-start) | async-done | bytes 262176 | tf_op jit(solution)/shard_map/all_to_all | solution.py:478
  205.3 0.7 copy-done.3
  206.0 6.5 %gradients.1 = (f32[4,1024,128]{2,1,0:T(8,128)}, f32[2,2,128]{2,1,0:T(2,128)}) custom-call(s32[1]{0:T(128)} %bitcast.y_ref, bf16[4,4,2,352,128]{4,3,2,1,0:T(8,128)(2,1)} %get-tuple-element.65.pack_ref, f32[4,4,2,2,8,128]{5,4,3,2,1,0:T(8,128)} %bitcast.39, f32[4,64,256]{2,1,0:T(8,128)} %get-tuple-element.81.gate_ref, ...), custom_call_target="tpu_custom_call" | custom-call | tf_op jit(solution)/shard_map/gradients/pallas_call | solution.py:398
  212.5 0.1 collective-permute-start.16
  212.6 0.8 slice_reduce_fusion
  213.3 0.6 reshape_squeeze.3
  213.9 3.0 %collective-permute-done.16.b_ref = f32[4,1024,128]{2,1,0:T(8,128)S(1)} collective-permute-done((f32[4,1024,128]{2,1,0:T(8,128)}, f32[4,1024,128]{2,1,0:T(8,128)S(1)}, u32[]{:S(2)}, u32[]{:S(2)}) %collective-permute-start.16) | collective-permute-done | bytes 2097184 | tf_op jit(solution)/shard_map/ppermute | solution.py:439
  216.9 1.3 copy-done.1
  218.3 3.2 %add_cores.1 = (f32[4,640,128]{2,1,0:T(8,128)}, f32[4,384,128]{2,1,0:T(8,128)}) custom-call(f32[4,1024,128]{2,1,0:T(8,128)} %get-tuple-element.89.a_ref, f32[4,1024,128]{2,1,0:T(8,128)} %copy-done.1), custom_call_target="tpu_custom_call" | custom-call | tf_op jit(solution)/shard_map/add_cores/pallas_call | solution.py:423
  (12 shorter events, 0.0 us)
Async XLA Ops:
  0.6 26.1 %collective-permute-start = (bf16[1024,512]{1,0:T(8,128)(2,1)}, bf16[1024,512]{1,0:T(8,128)(2,1)S(1)}, u32[]{:S(2)}, u32[]{:S(2)}) collective-permute-start(bf16[1024,512]{1,0:T(8,128)(2,1)} %bitcast.29), channel_id=1, source_target_pairs={{0,8},{8,16},{16,24},{24,0},{1,9},{9,17},{17,25},{25,1},{2,10},{10... | collective-permute-start | bytes 3145736 | tf_op jit(solution)/shard_map/ppermute | solution.py:435
  2.7 24.0 %collective-permute-start.1 = (bf16[1024,512]{1,0:T(8,128)(2,1)}, bf16[1024,512]{1,0:T(8,128)(2,1)S(1)}, u32[]{:S(2)}, u32[]{:S(2)}) collective-permute-start(bf16[1024,512]{1,0:T(8,128)(2,1)} %bitcast.30), channel_id=1, source_target_pairs={{0,24},{8,0},{16,8},{24,16},{1,25},{9,1},{17,9},{25,17},{2,26},{10... | collective-permute-start | bytes 3145736 | tf_op jit(solution)/shard_map/ppermute | solution.py:435
  4.1 30.6 %collective-permute-start.6 = (bf16[128,2560]{1,0:T(8,128)(2,1)}, bf16[128,2560]{1,0:T(8,128)(2,1)}, u32[]{:S(2)}, u32[]{:S(2)}) collective-permute-start(bf16[128,2560]{1,0:T(8,128)(2,1)} %bitcast.34), channel_id=1, source_target_pairs={{0,32},{32,64},{64,96},{96,0},{1,33},{33,65},{65,97},{97,1},{2,34}... | collective-permute-start | bytes 1966088 | tf_op jit(solution)/shard_map/ppermute | solution.py:435
  5.8 30.4 %collective-permute-start.7 = (bf16[128,2560]{1,0:T(8,128)(2,1)}, bf16[128,2560]{1,0:T(8,128)(2,1)}, u32[]{:S(2)}, u32[]{:S(2)}) collective-permute-start(bf16[128,2560]{1,0:T(8,128)(2,1)} %bitcast.35), channel_id=1, source_target_pairs={{0,96},{32,0},{64,32},{96,64},{1,97},{33,1},{65,33},{97,65},{2,98}... | collective-permute-start | bytes 1966088 | tf_op jit(solution)/shard_map/ppermute | solution.py:435
  8.0 29.1 %collective-permute-start.8 = (bf16[128,2560]{1,0:T(8,128)(2,1)}, bf16[128,2560]{1,0:T(8,128)(2,1)}, u32[]{:S(2)}, u32[]{:S(2)}) collective-permute-start(bf16[128,2560]{1,0:T(8,128)(2,1)} %bitcast.36), channel_id=1, source_target_pairs={{0,64},{32,96},{64,0},{96,32},{1,65},{33,97},{65,1},{97,33},{2,66}... | collective-permute-start | bytes 1966088 | tf_op jit(solution)/shard_map/ppermute | solution.py:435
  12.7 55.3 %copy-start = (bf16[1,1024,512]{2,1,0:T(8,128)(2,1)S(1)}, bf16[1,1024,512]{2,1,0:T(8,128)(2,1)}, u32[]{:S(2)}) copy-start(bf16[1,1024,512]{2,1,0:T(8,128)(2,1)} %param.7) | copy-start | bytes 3145732
  26.8 42.4 %copy-start.4 = (bf16[1024,512]{1,0:T(8,128)(2,1)}, bf16[1024,512]{1,0:T(8,128)(2,1)S(1)}, u32[]{:S(2)}) copy-start(bf16[1024,512]{1,0:T(8,128)(2,1)S(1)} %collective-permute-done.refs_1_) | copy-start | bytes 3145732
  26.8 42.4 %copy-start.5 = (bf16[1024,512]{1,0:T(8,128)(2,1)}, bf16[1024,512]{1,0:T(8,128)(2,1)S(1)}, u32[]{:S(2)}) copy-start(bf16[1024,512]{1,0:T(8,128)(2,1)S(1)} %collective-permute-done.1.refs_2_) | copy-start | bytes 3145732
  26.8 4.2 %collective-permute-start.2 = (bf16[352,128]{1,0:T(8,128)(2,1)}, bf16[352,128]{1,0:T(8,128)(2,1)S(1)}, u32[]{:S(2)}, u32[]{:S(2)}) collective-permute-start(bf16[352,128]{1,0:T(8,128)(2,1)} %pool.1), channel_id=1, source_target_pairs={{0,2},{2,0},{1,3},{3,1},{4,6},{6,4},{5,7},{7,5},{8,10},{10,8},{9,1... | collective-permute-start | bytes 270344 | tf_op jit(solution)/shard_map/ppermute | solution.py:439
  31.9 36.1 %collective-permute-start.3 = (bf16[2,352,128]{2,1,0:T(8,128)(2,1)S(1)}, bf16[2,352,128]{2,1,0:T(8,128)(2,1)S(1)}, u32[]{:S(2)}, u32[]{:S(2)}) collective-permute-start(bf16[2,352,128]{2,1,0:T(8,128)(2,1)S(1)} %pad_maximum_fusion.1), channel_id=1, source_target_pairs={{0,8},{8,16},{16,24},{24,0},{1,9},{9,17},{17,25},{25,1},{2,10},{10... | collective-permute-start | bytes 540680 | tf_op jit(solution)/shard_map/ppermute | solution.py:435
  32.9 35.0 %collective-permute-start.4 = (bf16[2,352,128]{2,1,0:T(8,128)(2,1)S(1)}, bf16[2,352,128]{2,1,0:T(8,128)(2,1)}, u32[]{:S(2)}, u32[]{:S(2)}) collective-permute-start(bf16[2,352,128]{2,1,0:T(8,128)(2,1)S(1)} %pad_maximum_fusion.1), channel_id=1, source_target_pairs={{0,24},{8,0},{16,8},{24,16},{1,25},{9,1},{17,9},{25,17},{2,26},{10... | collective-permute-start | bytes 540680 | tf_op jit(solution)/shard_map/ppermute | solution.py:435
  34.7 33.3 %collective-permute-start.5 = (bf16[2,352,128]{2,1,0:T(8,128)(2,1)S(1)}, bf16[2,352,128]{2,1,0:T(8,128)(2,1)}, u32[]{:S(2)}, u32[]{:S(2)}) collective-permute-start(bf16[2,352,128]{2,1,0:T(8,128)(2,1)S(1)} %pad_maximum_fusion.1), channel_id=1, source_target_pairs={{0,16},{8,24},{16,0},{24,8},{1,17},{9,25},{17,1},{25,9},{2,18},{10... | collective-permute-start | bytes 540680 | tf_op jit(solution)/shard_map/ppermute | solution.py:435
  68.0 55.2 %collective-permute-start.12 = (bf16[1024,512]{1,0:T(8,128)(2,1)S(1)}, bf16[1024,512]{1,0:T(8,128)(2,1)S(1)}, u32[]{:S(2)}, u32[]{:S(2)}) collective-permute-start(bf16[1024,512]{1,0:T(8,128)(2,1)S(1)} %bitcast.33), channel_id=1, source_target_pairs={{0,16},{8,24},{16,0},{24,8},{1,17},{9,25},{17,1},{25,9},{2,18},{10... | collective-permute-start | bytes 3145736 | tf_op jit(solution)/shard_map/ppermute | solution.py:435
  69.2 54.0 %copy-start.6 = (bf16[4,2,352,128]{3,2,1,0:T(8,128)(2,1)}, bf16[4,2,352,128]{3,2,1,0:T(8,128)(2,1)S(1)}, u32[]{:S(2)}) copy-start(bf16[4,2,352,128]{3,2,1,0:T(8,128)(2,1)S(1)} %pad_maximum_fusion.refs_0_) | copy-start | bytes 2162692
  69.2 69.4 %collective-permute-start.10 = (bf16[4,2,352,128]{3,2,1,0:T(8,128)(2,1)S(1)}, bf16[4,2,352,128]{3,2,1,0:T(8,128)(2,1)S(1)}, u32[]{:S(2)}, u32[]{:S(2)}) collective-permute-start(bf16[4,2,352,128]{3,2,1,0:T(8,128)(2,1)S(1)} %pad_maximum_fusion.refs_0_), channel_id=1, source_target_pairs={{0,64},{32,96},{64,0},{96,32},{1,65},{33,97},{65,1},{97,33},{2,66}... | collective-permute-start | bytes 2162696 | tf_op jit(solution)/shard_map/ppermute | solution.py:435
  69.3 69.4 %collective-permute-start.11 = (bf16[4,2,352,128]{3,2,1,0:T(8,128)(2,1)S(1)}, bf16[4,2,352,128]{3,2,1,0:T(8,128)(2,1)S(1)}, u32[]{:S(2)}, u32[]{:S(2)}) collective-permute-start(bf16[4,2,352,128]{3,2,1,0:T(8,128)(2,1)S(1)} %pad_maximum_fusion.refs_0_), channel_id=1, source_target_pairs={{0,32},{32,64},{64,96},{96,0},{1,33},{33,65},{65,97},{97,1},{2,34}... | collective-permute-start | bytes 2162696 | tf_op jit(solution)/shard_map/ppermute | solution.py:435
  69.4 69.3 %collective-permute-start.9 = (bf16[4,2,352,128]{3,2,1,0:T(8,128)(2,1)S(1)}, bf16[4,2,352,128]{3,2,1,0:T(8,128)(2,1)S(1)}, u32[]{:S(2)}, u32[]{:S(2)}) collective-permute-start(bf16[4,2,352,128]{3,2,1,0:T(8,128)(2,1)S(1)} %pad_maximum_fusion.refs_0_), channel_id=1, source_target_pairs={{0,96},{32,0},{64,32},{96,64},{1,97},{33,1},{65,33},{97,65},{2,98}... | collective-permute-start | bytes 2162696 | tf_op jit(solution)/shard_map/ppermute | solution.py:435
  123.2 1.0 copy-start.2
  136.0 12.0 %collective-permute-start.13 = (f32[4,5,2,512]{3,2,1,0:T(2,128)}, f32[4,5,2,512]{3,2,1,0:T(2,128)S(1)}, u32[]{:S(2)}, u32[]{:S(2)}) collective-permute-start(f32[4,5,2,512]{3,2,1,0:T(2,128)} %get-tuple-element.77.refs_3_), channel_id=1, source_target_pairs={{0,32},{32,64},{64,96},{96,0},{1,33},{33,65},{65,97},{97,1},{2,34}... | collective-permute-start | bytes 245768 | tf_op jit(solution)/shard_map/ppermute | solution.py:435
  136.0 12.0 %collective-permute-start.14 = (f32[4,5,2,512]{3,2,1,0:T(2,128)}, f32[4,5,2,512]{3,2,1,0:T(2,128)S(1)}, u32[]{:S(2)}, u32[]{:S(2)}) collective-permute-start(f32[4,5,2,512]{3,2,1,0:T(2,128)} %get-tuple-element.77.refs_3_), channel_id=1, source_target_pairs={{0,96},{32,0},{64,32},{96,64},{1,97},{33,1},{65,33},{97,65},{2,98}... | collective-permute-start | bytes 245768 | tf_op jit(solution)/shard_map/ppermute | solution.py:435
  138.7 0.9 copy-start.10
  138.7 9.3 %collective-permute-start.15 = (f32[4,5,2,512]{3,2,1,0:T(2,128)}, f32[4,5,2,512]{3,2,1,0:T(2,128)S(1)}, u32[]{:S(2)}, u32[]{:S(2)}) collective-permute-start(f32[4,5,2,512]{3,2,1,0:T(2,128)} %get-tuple-element.77.refs_3_), channel_id=1, source_target_pairs={{0,64},{32,96},{64,0},{96,32},{1,65},{33,97},{65,1},{97,33},{2,66}... | collective-permute-start | bytes 245768 | tf_op jit(solution)/shard_map/ppermute | solution.py:435
  138.7 1.1 copy-start.11
  139.8 0.9 copy-start.12
  148.0 0.6 copy-start.7
  148.0 0.6 copy-start.8
  148.0 0.7 copy-start.9
  152.3 53.0 %all-to-all-start = ((f32[32,2,8,128]{3,2,1,0:T(8,128)}), f32[32,2,8,128]{3,2,1,0:T(8,128)S(1)}, u32[]{:S(2)}, u32[]{:S(2)}) async-start(f32[32,2,8,128]{3,2,1,0:T(8,128)} %teacher.1), calls=%async_computation | async-start | bytes 524288 | tf_op jit(solution)/shard_map/all_to_all | solution.py:478
  205.3 0.7 copy-start.3
  212.5 4.5 %collective-permute-start.16 = (f32[4,1024,128]{2,1,0:T(8,128)}, f32[4,1024,128]{2,1,0:T(8,128)S(1)}, u32[]{:S(2)}, u32[]{:S(2)}) collective-permute-start(f32[4,1024,128]{2,1,0:T(8,128)} %get-tuple-element.89.a_ref), channel_id=1, source_target_pairs={{0,1},{1,0},{2,3},{3,2},{4,5},{5,4},{6,7},{7,6},{8,9},{9,8},{10,11... | collective-permute-start | bytes 6291464 | tf_op jit(solution)/shard_map/ppermute | solution.py:439
  216.9 1.3 copy-start.1
